TPU v7x, 32 devices: a whole 2x2x4 slice. The times are simulated.
32 devices in a mesh: exp: 8 (over z, core), ccd: 4 (over y, x).
Axes of the slice: x: 2, y: 2, z: 4, core: 2. Of those that a mesh axis runs over, the one named last changes fastest.
Arguments:
- pixels: bfloat16 [8, 4000, 4, 128], P('exp', 'ccd'), may hold values from -24 to 24
- psf_proj: bfloat16 [8, 100, 2160], P('ccd'), may hold values from -0.5 to 0.5
- resolution: float32 [200, 11, 512], P('ccd', None, 'exp'), may hold values from 0.02 to 0.16
- basis: float32 [10, 528], replicated, may hold values from -4 to 4
- sky_fibres: int32 [24], replicated, may hold values from 0 to 199, as said below
- fibre_slot: int32 [200], P('ccd'), may hold values from 0 to 199, as said below
- band_shift: int32 [200], P('ccd'), may hold values from -3 to 3
Outputs:
- sky_subtracted: float32 [8, 200, 512], P(None, 'ccd', 'exp')
- noise_rms: float32 [200, 512], P('ccd', 'exp')
Inputs may be any that keep to these rules, and one draw needn't show every extreme that they name: `sky_fibres`: 24 distinct fibre numbers, listed group by group: entries g * 6 to (g + 1) * 6 - 1 are fibres of the group g of 50 consecutive fibres. `fibre_slot`: for each group g of 50 consecutive fibres, a permutation of the slots g * 50 to (g + 1) * 50 - 1.
All inputs are finite; a program needn't handle non-finite values.
Results may differ from a plain program's by a relative error of at most 0.00095.
Values may be sent and summed in bfloat16 or wider, within the bound.
A program may use at most 64 MiB of HBM per device.

v0:
```python
import jax
import jax.numpy as jnp
from jax import lax
from jax.sharding import PartitionSpec as P

BPIX = 500
MARG = 20
ROWS = 4
BAND = 11
SHIFT = 3
FC = 50
SPAN = 540


highest = lax.Precision.HIGHEST


def extended(x, sides, width):
    for axis, dim in sides:
        size, length = (lax.axis_size(axis), x.shape[dim])
        up = [(i, (i + 1) % size) for i in range(size - 1)]
        down = [(j, i) for i, j in up]
        last = lax.slice_in_dim(x, length - width, length, axis=dim)
        leading = lax.slice_in_dim(x, 0, width, axis=dim)
        before = lax.ppermute(last, axis, up)
        after = lax.ppermute(leading, axis, down)
        x = jnp.concatenate([before, x, after], axis=dim)
    return x


def band_model(pieces, spectra, shifts):
    length = pieces.shape[2]

    def window_of(shift):
        return lax.dynamic_slice(
            spectra, (jnp.int32(0), shift + SHIFT), (spectra.shape[0], length + BAND - 1)
        )

    windows = jax.vmap(window_of)(shifts)
    total = jnp.zeros((pieces.shape[0], spectra.shape[0], length), jnp.float32)
    for offset in range(BAND):
        total = total + pieces[:, offset, None, :] * windows[:, :, offset : offset + length]
    return total


def solve_small(gram, target):
    factor = jnp.linalg.cholesky(gram)
    return jax.scipy.linalg.cho_solve((factor, True), target[..., None])[..., 0]


def shards(pixels, psf_proj, resolution, basis, sky_fibres, fibre_slot, band_shift):
    padded = extended(pixels, (("ccd", 1),), MARG)
    pixvar = (0.25 + jnp.square(padded.astype(jnp.float32))).astype(jnp.bfloat16)
    proj_square = jnp.square(psf_proj.astype(jnp.float32)).astype(jnp.bfloat16)
    groups = pixels.shape[3]
    flux_parts = []
    var_parts = []
    for block in range(psf_proj.shape[0]):
        lower = block * BPIX
        window = padded[0, lower : lower + SPAN].reshape(SPAN * ROWS, groups)
        window_var = pixvar[0, lower : lower + SPAN].reshape(SPAN * ROWS, groups)
        flux_parts.append(jnp.dot(psf_proj[block], window, preferred_element_type=jnp.float32))
        var_parts.append(
            jnp.dot(proj_square[block], window_var, preferred_element_type=jnp.float32)
        )
    flux_slots = jnp.concatenate(flux_parts, 0).reshape(FC, ROWS * groups)
    var_slots = jnp.concatenate(var_parts, 0).reshape(FC, ROWS * groups)
    group_base = lax.axis_index("ccd") * FC
    local_slot = fibre_slot - group_base
    flux_rows = jnp.take(flux_slots, local_slot, axis=0)
    var_rows = jnp.take(var_slots, local_slot, axis=0)
    fibre_ids = group_base + jnp.arange(FC, dtype=jnp.int32)
    skymask = jnp.any(fibre_ids[:, None] == sky_fibres[None, :], axis=1).astype(jnp.float32)
    model = band_model(
        lax.all_gather(resolution.astype(jnp.bfloat16), "exp", axis=2, tiled=True).astype(
            jnp.float32
        ),
        basis,
        band_shift,
    )
    weight = skymask[:, None] / var_rows
    weighted = model * weight[:, None, :]
    gram = jnp.einsum("fkw,flw->kl", weighted, model, precision=highest)
    target = jnp.einsum("fkw,fw->k", weighted, flux_rows, precision=highest)
    gram, target = lax.psum((gram, target), "ccd")
    coeffs = solve_small(gram, target)
    residual = flux_rows - jnp.einsum("k,fkw->fw", coeffs, model, precision=highest)
    sky_subtracted = lax.all_to_all(residual[None], "exp", split_axis=2, concat_axis=0, tiled=True)
    centred = sky_subtracted - jnp.mean(sky_subtracted, axis=0)
    noise_rms = jnp.sqrt(jnp.mean(jnp.square(centred), axis=0) + 1e-06)
    return (sky_subtracted, noise_rms)


def solution(mesh):
    in_specs = (
        P("exp", "ccd", None, None),
        P("ccd", None, None),
        P("ccd", None, "exp"),
        P(),
        P(),
        P("ccd"),
        P("ccd"),
    )
    out_specs = (P(None, "ccd", "exp"), P("ccd", "exp"))
    return jax.shard_map(shards, mesh=mesh, in_specs=in_specs, out_specs=out_specs, check_vma=False)
```

profile of v0, /device:TPU:0, one launch (start us, length us, event | category | flops | bytes accessed | tf_op | source)
XLA Modules:
  0.0 163.1 jit_solution(1939517801104536074)
XLA Ops:
  0.6 1.4 fusion.24
  2.0 4.8 %collective-permute-start = (bf16[1,20,4,128]{3,2,1,0:T(4,128)(2,1)}, bf16[1,20,4,128]{3,2,1,0:T(4,128)(2,1)S(1)}, u32[]{:S(2)}, u32[]{:S(2)}) collective-permute-start(bf16[1,20,4,128]{3,2,1,0:T(4,128)(2,1)} %get-tuple-element.38), channel_id=1, source_target_pairs={{0,1},{1,2},{2,3},{4,5},{5,6},{6,7},{8,9},{9,10},{10,11},{12,13},{... | collective-permute-start | bytes 61448 | tf_op jit(solution)/shard_map/ppermute | solution.py:25
  6.8 1.3 collective-permute-start.1
  8.2 1.0 convert_element_type.41
  9.4 23.7 %all_gather.3 = bf16[50,11,512]{0,1,2:T(8,128)(2,1)S(1)} all-gather(bf16[50,11,64]{0,1,2:T(8,128)(2,1)S(1)} %copy.60), channel_id=1, replica_groups=mesh['exp'=8,'ccd'=4] {'exp'}, dimensions={2}, use_global_device_ids=true | all-gather | bytes 633600 | tf_op jit(solution)/shard_map/all_gather | solution.py:75
  33.1 3.0 %fusion.22 = (f32[50,1,512]{0,1,2:T(1,128)}, f32[50,1,512]{0,1,2:T(1,128)}, f32[50,1,512]{0,1,2:T(1,128)}, f32[50,1,512]{0,1,2:T(1,128)}, f32[50,1,512]{0,1,2:T(...) fusion(bf16[50,11,512]{0,1,2:T(8,128)(2,1)S(1)} %all_gather.3), kind=kLoop, calls=%fused_computation.56 | loop fusion | bytes 2252800 | tf_op jit(solution)/shard_map/slice | solution.py:42
  36.2 1.1 copy.61
  37.2 1.7 %copy.62 = f32[50,512]{1,0:T(8,128)} copy(f32[50,512]{0,1:T(8,128)} %bitcast.105) | data formatting | bytes 204800 | tf_op jit(solution)/shard_map/mul | solution.py:42
  39.0 1.7 %copy.63 = f32[50,512]{1,0:T(8,128)} copy(f32[50,512]{0,1:T(8,128)} %bitcast.104) | data formatting | bytes 204800 | tf_op jit(solution)/shard_map/mul | solution.py:42
  40.7 1.7 %copy.64 = f32[50,512]{1,0:T(8,128)} copy(f32[50,512]{0,1:T(8,128)} %bitcast.103) | data formatting | bytes 204800 | tf_op jit(solution)/shard_map/mul | solution.py:42
  42.4 1.7 %copy.65 = f32[50,512]{1,0:T(8,128)} copy(f32[50,512]{0,1:T(8,128)} %bitcast.102) | data formatting | bytes 204800 | tf_op jit(solution)/shard_map/mul | solution.py:42
  44.1 1.7 %copy.66 = f32[50,512]{1,0:T(8,128)} copy(f32[50,512]{0,1:T(8,128)} %bitcast.101) | data formatting | bytes 204800 | tf_op jit(solution)/shard_map/mul | solution.py:42
  45.9 0.8 copy.67
  46.6 0.8 copy.68
  47.4 0.8 copy.69
  48.2 0.8 copy.70
  49.0 0.8 copy.71
  50.4 61.5 %while.1 = (s32[]{:T(128)}, f32[10,528]{1,0:T(8,128)S(1)}, s32[50,2]{0,1:T(2,128)S(1)}, f32[50,10,522]{2,1,0:T(8,128)S(1)}, s32[]{:T(128)}) while((s32[]{:T(128)}, f32[10,528]{1,0:T(8,128)S(1)}, s32[50,2]{0,1:T(2,128)S(1)}, f32[50,10,522]{2,1,0:T(8,128)S(1)}, s32[]{:T(128)}) %tuple.39), condition=%wide.while_cond, body=%wide.while_body.sunk | while | flops 2 | bytes 82017 | solution.py:35
  112.0 1.4 multiply_convert_fusion
  113.6 6.5 %multiply_add_fusion = f32[50,10,512]{2,1,0:T(8,128)} fusion(f32[50,10,522]{2,1,0:T(8,128)S(1)} %get-tuple-element.10, f32[50,512]{1,0:T(8,128)S(1)} %copy-done.10, f32[50,512]{1,0:T(8,128)S(1)} %copy-done.9, f32[50,512]{1,0:T(8,128)S(1)} %copy-done.8, f32[50,512]{1,0:T(8,128)} %copy.68, f32[50,512]{1,0:T(8,128)} %copy.67, f32[50,512]{1,0:T(8,128)} %copy.66, ...), kind=kLoop, calls=%fused_computation.10 | loop fusion | flops 5376000 | bytes 13414400 | tf_op jit(solution)/shard_map/add | solution.py:42
  120.2 1.1 copy-done.1
  121.2 0.7 pad_maximum_fusion.1
  122.6 3.9 %add_convert_fusion = bf16[1,1040,4,128]{3,2,1,0:T(4,128)(2,1)S(1)} fusion(bf16[1,20,4,128]{3,2,1,0:T(4,128)(2,1)S(1)} %collective-permute-done.1, bf16[1,1000,4,128]{3,2,1,0:T(4,128)(2,1)S(1)} %copy-done.1, bf16[1,20,4,128]{3,2,1,0:T(4,128)(2,1)S(1)} %collective-permute-done), kind=kLoop, calls=%fused_computation.8 | loop fusion | flops 3194880 | bytes 2129920 | tf_op jit(solution)/shard_map/convert_element_type | solution.py:53
  128.9 2.3 %fusion.4 = f32[10,10]{0,1:T(8,128)S(1)} fusion(f32[50,10,512]{2,1,0:T(8,128)S(1)} %copy-done, f32[50,512]{1,0:T(8,128)S(1)} %get-tuple-element.41), kind=kOutput, calls=%fused_computation.13 | convolution fusion | flops 30976000 | bytes 1126800 | tf_op jit(solution)/shard_map/fkw,flw->kl/dot_general | solution.py:83
  131.2 2.0 %fusion.7 = f32[10]{0:T(128)S(1)} fusion(f32[50,10,512]{2,1,0:T(8,128)S(1)} %copy-done, f32[50,512]{1,0:T(8,128)S(1)} %get-tuple-element.41, f32[50,512,1]{1,0,2:T(8,128)S(1)} %get-tuple-element.40), kind=kOutput, calls=%fused_computation.14 | convolution fusion | flops 3328000 | bytes 1228840 | tf_op jit(solution)/shard_map/fkw,fw->k/dot_general | solution.py:84
  133.3 11.4 %all-reduce.1 = (f32[10,10]{0,1:T(8,128)S(1)}, f32[10]{0:T(128)S(1)}) all-reduce(f32[10,10]{0,1:T(8,128)S(1)} %fusion.4, f32[10]{0:T(128)S(1)} %fusion.7), channel_id=1, replica_groups=mesh['exp'=8,'ccd'=4] {'ccd'}, use_global_device_ids=true, to_apply=%region_1.3 | all-reduce | flops 110 | bytes 880 | tf_op jit(solution)/shard_map/psum | solution.py:85
  144.8 0.9 cholesky.16
  147.0 0.8 custom-call.10
  148.1 0.9 fusion.25
  149.8 1.3 reduce.7
  151.4 9.4 %all_to_all.18 = f32[8,1,3200]{2,1,0:T(1,128)S(1)} all-to-all(f32[8,1,3200]{2,1,0:T(1,128)S(1)} %reshape.151), channel_id=1, replica_groups=mesh['exp'=8,'ccd'=4] {'exp'}, dimensions={0} | all-to-all | bytes 204800 | tf_op jit(solution)/shard_map/all_to_all | solution.py:88
  160.8 0.9 reduce.8
  (216 shorter events, 69.7 us)
Async XLA Ops:
  2.0 118.2 %collective-permute-start = (bf16[1,20,4,128]{3,2,1,0:T(4,128)(2,1)}, bf16[1,20,4,128]{3,2,1,0:T(4,128)(2,1)S(1)}, u32[]{:S(2)}, u32[]{:S(2)}) collective-permute-start(bf16[1,20,4,128]{3,2,1,0:T(4,128)(2,1)} %get-tuple-element.38), channel_id=1, source_target_pairs={{0,1},{1,2},{2,3},{4,5},{5,6},{6,7},{8,9},{9,10},{10,11},{12,13},{... | collective-permute-start | bytes 61448 | tf_op jit(solution)/shard_map/ppermute | solution.py:25
  6.8 113.3 %collective-permute-start.1 = (bf16[1,20,4,128]{3,2,1,0:T(4,128)(2,1)}, bf16[1,20,4,128]{3,2,1,0:T(4,128)(2,1)S(1)}, u32[]{:S(2)}, u32[]{:S(2)}) collective-permute-start(bf16[1,20,4,128]{3,2,1,0:T(4,128)(2,1)} %get-tuple-element.39), channel_id=1, source_target_pairs={{1,0},{2,1},{3,2},{5,4},{6,5},{7,6},{9,8},{10,9},{11,10},{13,12},{... | collective-permute-start | bytes 61448 | tf_op jit(solution)/shard_map/ppermute | solution.py:26
  39.0 11.5 %copy-start.4 = (f32[10,528]{1,0:T(8,128)S(1)}, f32[10,528]{1,0:T(8,128)}, u32[]{:S(2)}) copy-start(f32[10,528]{1,0:T(8,128)} %param.12) | copy-start | bytes 63364
  46.6 65.3 %copy-start.11 = (s32[50]{0:T(128)S(1)}, s32[50]{0:T(128)}, u32[]{:S(2)}) copy-start(s32[50]{0:T(128)} %param.14) | copy-start | bytes 604
  48.2 65.2 %copy-start.12 = (s32[24]{0:T(128)S(1)}, s32[24]{0:T(128)}, u32[]{:S(2)}) copy-start(s32[24]{0:T(128)} %param.13) | copy-start | bytes 292
  48.2 65.3 %copy-start.5 = (f32[50,512]{1,0:T(8,128)S(1)}, f32[50,512]{1,0:T(8,128)}, u32[]{:S(2)}) copy-start(f32[50,512]{1,0:T(8,128)} %copy.62) | copy-start | bytes 307204
  48.2 65.3 %copy-start.6 = (f32[50,512]{1,0:T(8,128)S(1)}, f32[50,512]{1,0:T(8,128)}, u32[]{:S(2)}) copy-start(f32[50,512]{1,0:T(8,128)} %copy.63) | copy-start | bytes 307204
  48.2 65.3 %copy-start.7 = (f32[50,512]{1,0:T(8,128)S(1)}, f32[50,512]{1,0:T(8,128)}, u32[]{:S(2)}) copy-start(f32[50,512]{1,0:T(8,128)} %copy.64) | copy-start | bytes 307204
  111.9 1.6 copy-start.8
  111.9 1.6 copy-start.9
  112.0 1.6 copy-start.10
  113.5 6.5 %copy-start.2 = (bf16[2,100,2160]{2,0,1:T(2,128)(2,1)S(1)}, bf16[2,100,2160]{2,0,1:T(2,128)(2,1)}, u32[]{:S(2)}) copy-start(bf16[2,100,2160]{2,0,1:T(2,128)(2,1)} %param.10) | copy-start | bytes 2592004
  120.0 1.2 copy-start.1
  127.5 1.4 copy-start
  162.3 0.8 copy-start.3
where the time goes:
time: 166 us; the launch traced here: 163 us
  local copies, waits for them, and re-layouts  84.2 us (51%)
  blocking collectives  44.5 us (27%)
  other arithmetic  20.4 us (12%)
  matrix products  6.68 us (4%)
  starting transfers between devices  6.12 us (4%)
    gather x150, local copies, waits for them, and re-layouts  61.4 us
    all_gather x1, blocking collectives, shards(): lax.all_gather(resolution.astype(jnp.bfloat16), 'exp', axis=2, tiled=True)  23.7 us
    mul x11, local copies, waits for them, and re-layouts, band_model(): pieces[:, offset, None, :] * windows[:, :, offset:offset + length]  13.6 us
    psum x1, blocking collectives, shards(): gram, target = lax.psum((gram, target), 'ccd')  11.4 us
    all_to_all x1, blocking collectives, shards(): lax.all_to_all(residual[None], 'exp', split_axis=2, concat_axis=0, tiled=...  9.43 us
    add x1, other arithmetic, band_model(): total + pieces[:, offset, None, :] * windows[:, :, offset:offset + length]  6.47 us
    ppermute x1, starting transfers between devices, extended(): before = lax.ppermute(last, axis, up)  4.83 us
    convert_element_type x1, other arithmetic, shards(): (0.25 + jnp.square(padded.astype(jnp.float32))).astype(jnp.bfloat16)  3.93 us
  transfers between devices with their start and end apart: 2, of which 0 were waited for; matrix products, arithmetic and copies ran while one was open for 54% of the time, Pallas kernels for 0%

commit v1 on v0

v1 whole, which is shorter than its diff:
```python
import functools

import jax
import jax.numpy as jnp
from jax import lax
from jax.experimental import pallas as pl
from jax.experimental.pallas import tpu as pltpu
from jax.sharding import PartitionSpec as P

BPIX = 500
MARG = 20
ROWS = 4
BAND = 11
SHIFT = 3
SPAN = 540
LANES = 128
TAPS = BAND + 2 * SHIFT
HALO = MARG * ROWS
DEEP = SPAN * ROWS
SLOTS = 64
SKYROW = 56
MESH = pl.DeviceIdType.MESH


def column_of(row, count):
    n = row.shape[1]
    sub = lax.broadcasted_iota(jnp.int32, (count, n), 0)
    lane = lax.broadcasted_iota(jnp.int32, (count, n), 1)
    return jnp.sum(jnp.where(sub == lane, row, 0), axis=1, keepdims=True)


def pieces_of(x):
    high = x.astype(jnp.bfloat16)
    rest = x - high.astype(jnp.float32)
    mid = rest.astype(jnp.bfloat16)
    low = (rest - mid.astype(jnp.float32)).astype(jnp.bfloat16)
    return high, mid, low


def kernel(
    n_e, n_c, skyc, comp,
    pix_hbm, psf_hbm, res_hbm, basis_ref, slot_row, shift_row, sky_s, slot_s, shift_s,
    out_ref, rms_ref,
    xs, psf, res, res2, bpad, bsh, stage, skysend, skyrecv, skyfull, slots, fluxr,
    fsend, frecv, grecv, csend, crecv, croll, outs,
    local_sem, halo_ssem, halo_rsem, sky_ssem, sky_rsem, f_ssem, f_rsem,
    g_ssem, g_rsem, c_ssem, c_rsem,
):
    me = lax.axis_index("exp")
    mc = lax.axis_index("ccd")
    fc = res.shape[1]
    wl = res.shape[2]
    own = pix_hbm.shape[0]
    groups = LANES // wl
    tall = SLOTS // groups
    per = stage.shape[0]
    half = psf.shape[1]
    f32 = jnp.float32

    get_res = pltpu.make_async_copy(res_hbm, res, local_sem.at[0])
    get_psf = pltpu.make_async_copy(psf_hbm, psf, local_sem.at[1])
    get_pix = pltpu.make_async_copy(pix_hbm, xs.at[pl.ds(HALO, own)], local_sem.at[2])
    get_res.start()
    get_psf.start()
    get_pix.start()

    barrier = pltpu.get_barrier_semaphore()
    for d in range(1, n_e):
        pl.semaphore_signal(
            barrier, inc=1, device_id={"exp": lax.rem(me + d, n_e)}, device_id_type=MESH
        )
    for d in range(1, n_c):
        pl.semaphore_signal(
            barrier, inc=1, device_id={"ccd": lax.rem(mc + d, n_c)}, device_id_type=MESH
        )

    sky = [jnp.clip(sky_s[mc * skyc + i] - mc * fc, 0, fc - 1) for i in range(skyc)]

    stage[...] = jnp.zeros_like(stage)
    bpad[...] = jnp.zeros_like(bpad)
    bpad[0:comp, 0 : basis_ref.shape[1]] = basis_ref[...]
    get_res.wait()
    for i in range(skyc):
        q, s = i // per, i % per
        for d in range(BAND):
            stage[s, d : d + 1, q * wl : (q + 1) * wl] = res[d, pl.ds(sky[i], 1), :]
    skysend[...] = stage[...].astype(jnp.bfloat16)

    pl.semaphore_wait(barrier, n_e - 1 + n_c - 1)

    def to_left():
        return pltpu.make_async_remote_copy(
            src_ref=pix_hbm.at[pl.ds(0, HALO)],
            dst_ref=xs.at[pl.ds(HALO + own, HALO)],
            send_sem=halo_ssem.at[0],
            recv_sem=halo_rsem.at[0],
            device_id={"ccd": lax.rem(mc + n_c - 1, n_c)},
            device_id_type=MESH,
        )

    def to_right():
        return pltpu.make_async_remote_copy(
            src_ref=pix_hbm.at[pl.ds(own - HALO, HALO)],
            dst_ref=xs.at[pl.ds(0, HALO)],
            send_sem=halo_ssem.at[1],
            recv_sem=halo_rsem.at[1],
            device_id={"ccd": lax.rem(mc + 1, n_c)},
            device_id_type=MESH,
        )

    @pl.when(mc > 0)
    def _():
        to_left().start()

    @pl.when(mc < n_c - 1)
    def _():
        to_right().start()

    @pl.when(mc == 0)
    def _():
        xs[0:HALO, :] = jnp.zeros((HALO, LANES), xs.dtype)

    @pl.when(mc == n_c - 1)
    def _():
        xs[HALO + own :, :] = jnp.zeros((HALO, LANES), xs.dtype)

    def exchange(axis, size, mine, source, landing, ssem, rsem):
        sends, receives = [], []
        for d in range(1, size):
            there = lax.rem(mine + d, size)
            origin = lax.rem(mine + size - d, size)
            sends.append(
                pltpu.make_async_remote_copy(
                    src_ref=source(there), dst_ref=landing.at[mine],
                    send_sem=ssem.at[d], recv_sem=rsem.at[mine],
                    device_id={axis: there}, device_id_type=MESH,
                )
            )
            receives.append(
                pltpu.make_async_remote_copy(
                    src_ref=source(there), dst_ref=landing.at[origin],
                    send_sem=ssem.at[d], recv_sem=rsem.at[origin],
                    device_id={axis: there}, device_id_type=MESH,
                )
            )
        return sends, receives

    sky_out, sky_in = exchange(
        "exp", n_e, me, lambda there: skysend, skyrecv, sky_ssem, sky_rsem
    )
    for copy in sky_out:
        copy.start()
    skyrecv[me] = skysend[...]

    wide = bsh.shape[2]
    for e in range(TAPS):
        bsh[e] = bpad[:, e : e + wide]

    slot = column_of(slot_row[...], SLOTS) - mc * fc
    place = lax.broadcasted_iota(jnp.int32, (SLOTS, 1), 0)
    slot = jnp.where(place < fc, slot, -1000)
    for i in range(skyc):
        slot = jnp.where(place == SKYROW + i, slot_s[sky[i]] - mc * fc, slot)
    gap = slots.shape[0] // 2 - half
    first = slot * ROWS + jnp.where(slot * ROWS >= half, gap, 0)
    lane = lax.broadcasted_iota(jnp.int32, (SLOTS, slots.shape[0]), 1)
    pick = jnp.concatenate(
        [jnp.where(lane == first + r, 1.0, 0.0) for r in range(ROWS)], axis=0
    ).astype(jnp.bfloat16)

    slots[...] = jnp.zeros_like(slots)
    get_psf.wait()
    get_pix.wait()

    def partial(block, lower, upper):
        weights = psf[block, :, lower:upper]
        start = block * BPIX * ROWS
        window = xs[start + lower : start + upper, :]
        wide_w = weights.astype(f32)
        wide_x = window.astype(f32)
        squares = (wide_w * wide_w).astype(jnp.bfloat16)
        pixvar = (0.25 + wide_x * wide_x).astype(jnp.bfloat16)
        flux = jnp.dot(weights, window, preferred_element_type=f32)
        var = jnp.dot(squares, pixvar, preferred_element_type=f32)
        return flux, var

    blocks = psf.shape[0]
    cuts = []
    for b in range(blocks):
        lower = LANES if b == 0 else 0
        upper = (DEEP - HALO) // LANES * LANES if b == blocks - 1 else DEEP
        cuts.append((lower, upper))
    main = [partial(b, *cuts[b]) for b in range(blocks)]

    @pl.when(mc < n_c - 1)
    def _():
        to_left().wait_recv()

    @pl.when(mc > 0)
    def _():
        to_right().wait_recv()

    pitch = slots.shape[0] // 2
    for b in range(blocks):
        flux, var = main[b]
        lower, upper = cuts[b]
        if lower > 0:
            more = partial(b, 0, lower)
            flux, var = flux + more[0], var + more[1]
        if upper < DEEP:
            more = partial(b, upper, DEEP)
            flux, var = flux + more[0], var + more[1]
        slots[b * pitch : b * pitch + half, 0:LANES] = flux
        slots[b * pitch : b * pitch + half, LANES:] = var

    high, mid, low = pieces_of(slots[...])
    dot = functools.partial(jnp.dot, preferred_element_type=f32)
    chosen = dot(pick, high) + (dot(pick, mid) + dot(pick, low))
    fluxr[...] = chosen

    for j in range(n_e):
        r, off = j * wl // LANES, j * wl % LANES
        for q in range(groups):
            rows = pl.ds(r * SLOTS + q * tall, tall)
            fsend[j, :, q * wl : (q + 1) * wl] = fluxr[rows, off : off + wl]
    f_out, f_in = exchange(
        "exp", n_e, me, lambda there: fsend.at[there], frecv, f_ssem, f_rsem
    )
    for copy in f_out:
        copy.start()
    frecv[me] = fsend[me]

    for copy in sky_in:
        copy.wait_recv()
    for j in range(n_e):
        block = skyrecv[j].astype(f32)
        for i in range(skyc):
            q, s = i // per, i % per
            skyfull[i, :, j * wl : (j + 1) * wl] = block[s, :, q * wl : (q + 1) * wl]
    sub = lax.broadcasted_iota(jnp.int32, (16, wide), 0)
    sums = [jnp.zeros((16, LANES), f32) for _ in range(comp + 1)]
    for i in range(skyc):
        offset = jnp.clip(shift_s[sky[i]] + SHIFT, 0, 2 * SHIFT)
        model = jnp.zeros((16, wide), f32)
        for d in range(BAND):
            model = model + skyfull[i, d : d + 1, :] * bsh[offset + d]
        rows = [r * SLOTS + SKYROW + i for r in range(ROWS)]
        flux = jnp.concatenate([fluxr[x : x + 1, 0:LANES] for x in rows], axis=1)
        var = jnp.concatenate([fluxr[x : x + 1, LANES:] for x in rows], axis=1)
        full = jnp.where(sub == comp, flux, model)
        weighted = full * (1.0 / var)
        for col in range(comp + 1):
            product = weighted * full[col : col + 1, :]
            for t in range(0, wide, LANES):
                sums[col] = sums[col] + product[:, t : t + LANES]
    lanes16 = lax.broadcasted_iota(jnp.int32, (16, LANES), 1)
    sub16 = lax.broadcasted_iota(jnp.int32, (16, LANES), 0)
    gram = jnp.zeros((16, LANES), f32)
    for col in range(comp + 1):
        gram = jnp.where(lanes16 == col, jnp.sum(sums[col], axis=1, keepdims=True), gram)
    grecv[mc] = gram
    g_out, g_in = exchange(
        "ccd", n_c, mc, lambda there: grecv.at[mc], grecv, g_ssem, g_rsem
    )
    for copy in g_out:
        copy.start()

    planes = [res[d] for d in range(BAND)]
    shift = column_of(shift_row[...], fc) + SHIFT
    for step in (1, 2, 4):
        take = jnp.bitwise_and(shift, step) != 0
        length = min(len(planes) + step, TAPS)
        moved = []
        for e in range(length):
            here = planes[e] if e < len(planes) else jnp.zeros((fc, wl), f32)
            before = planes[e - step] if e >= step else jnp.zeros((fc, wl), f32)
            moved.append(jnp.where(take, before, here))
        planes = moved
    for e in range(TAPS):
        res2[e] = planes[e]

    for copy in g_in:
        copy.wait_recv()
    m = grecv[0]
    for c in range(1, n_c):
        m = m + grecv[c]
    for k in range(comp):
        row = m[k : k + 1, :] / m[k : k + 1, k : k + 1]
        m = jnp.where(sub16 == k, row, m - m[:, k : k + 1] * row)
    coeffs = jnp.where(sub16[:, 0:1] < comp, m[:, comp : comp + 1], 0.0)
    spectrum = jnp.sum(coeffs * bpad[...], axis=0, keepdims=True)
    for j in range(n_e):
        csend[j] = spectrum[:, j * wl : j * wl + LANES]
    c_out, c_in = exchange(
        "exp", n_e, me, lambda there: csend.at[there], crecv, c_ssem, c_rsem
    )
    for copy in c_out:
        copy.start()
    crecv[me] = csend[me]
    for copy in f_in:
        copy.wait_recv()
    for copy in c_in:
        copy.wait_recv()

    fitted = jnp.concatenate([crecv[e] for e in range(n_e)], axis=0)
    for e in range(TAPS):
        croll[e] = fitted if e == 0 else pltpu.roll(fitted, LANES - e, 1)

    for q in range(groups):
        base = q * tall
        count = min(tall, fc - base)
        if count <= 0:
            continue
        total = jnp.zeros((count, wl), f32)
        for e in range(n_e):
            glow = jnp.zeros((count, wl), f32)
            for t in range(TAPS):
                glow = glow + res2[t, base : base + count, :] * croll[t, e : e + 1, 0:wl]
            left = frecv[e, 0:count, q * wl : (q + 1) * wl] - glow
            outs[e, base : base + count, :] = left
            total = total + left
        mean = total / n_e
        square = jnp.zeros((count, wl), f32)
        for e in range(n_e):
            gone = outs[e, base : base + count, :] - mean
            square = square + gone * gone
        rms_ref[base : base + count, :] = jnp.sqrt(square / n_e + 1e-06)
    out_ref[...] = jnp.swapaxes(outs[...], 0, 1)

    @pl.when(mc > 0)
    def _():
        to_left().wait_send()

    @pl.when(mc < n_c - 1)
    def _():
        to_right().wait_send()

    for copy in sky_out + f_out + g_out + c_out:
        copy.wait_send()


def shards(n_e, n_c, pixels, psf_proj, resolution, basis, sky_fibres, fibre_slot, band_shift):
    fc, band, wl = resolution.shape
    comp, ext = basis.shape
    skyc = sky_fibres.shape[0] // n_c
    own = pixels.shape[1] * pixels.shape[2]
    wave = wl * n_e
    groups = LANES // wl
    per = -(-skyc // groups)
    half = psf_proj.shape[1]
    pitch = -(-half // 8) * 8
    f32, bf16 = jnp.float32, jnp.bfloat16
    anywhere = pl.BlockSpec(memory_space=pl.ANY)
    vmem = pl.BlockSpec(memory_space=pltpu.VMEM)
    smem = pl.BlockSpec(memory_space=pltpu.SMEM)
    dma = pltpu.SemaphoreType.DMA
    scratch = [
        pltpu.VMEM((own + 2 * HALO, LANES), bf16),
        pltpu.VMEM(psf_proj.shape, bf16),
        pltpu.VMEM((band, fc, wl), f32),
        pltpu.VMEM((TAPS, fc, wl), f32),
        pltpu.VMEM((16, wave + LANES), f32),
        pltpu.VMEM((TAPS, 16, wave), f32),
        pltpu.VMEM((per, 16, LANES), f32),
        pltpu.VMEM((per, 16, LANES), bf16),
        pltpu.VMEM((n_e, per, 16, LANES), bf16),
        pltpu.VMEM((skyc, 16, wave), f32),
        pltpu.VMEM((2 * pitch, 2 * LANES), f32),
        pltpu.VMEM((ROWS * SLOTS, 2 * LANES), f32),
        pltpu.VMEM((n_e, SLOTS // groups, LANES), f32),
        pltpu.VMEM((n_e, SLOTS // groups, LANES), f32),
        pltpu.VMEM((n_c, 16, LANES), f32),
        pltpu.VMEM((n_e, 1, LANES), f32),
        pltpu.VMEM((n_e, 1, LANES), f32),
        pltpu.VMEM((TAPS, n_e, LANES), f32),
        pltpu.VMEM((n_e, fc, wl), f32),
        dma((3,)),
        dma((2,)),
        dma((2,)),
    ]
    for size in (n_e, n_e, n_c, n_e):
        scratch += [dma((size,)), dma((size,))]
    cube, rms = pl.pallas_call(
        functools.partial(kernel, n_e, n_c, skyc, comp),
        out_shape=(
            jax.ShapeDtypeStruct((fc, n_e, wl), f32),
            jax.ShapeDtypeStruct((fc, wl), f32),
        ),
        in_specs=[anywhere, anywhere, anywhere, vmem, vmem, vmem, smem, smem, smem],
        out_specs=(vmem, vmem),
        scratch_shapes=scratch,
        compiler_params=pltpu.CompilerParams(
            collective_id=0, has_side_effects=True, vmem_limit_bytes=32 * 1024 * 1024
        ),
        name="extract",
    )(
        pixels.reshape(own, LANES),
        psf_proj,
        jnp.swapaxes(resolution, 0, 1),
        basis,
        fibre_slot.reshape(1, fc),
        band_shift.reshape(1, fc),
        sky_fibres,
        fibre_slot,
        band_shift,
    )
    return jnp.swapaxes(cube, 0, 1), rms


def solution(mesh):
    in_specs = (
        P("exp", "ccd", None, None),
        P("ccd", None, None),
        P("ccd", None, "exp"),
        P(),
        P(),
        P("ccd"),
        P("ccd"),
    )
    out_specs = (P(None, "ccd", "exp"), P("ccd", "exp"))
    body = functools.partial(shards, mesh.shape["exp"], mesh.shape["ccd"])
    return jax.shard_map(body, mesh=mesh, in_specs=in_specs, out_specs=out_specs, check_vma=False)
```

time: 166 us -> 24.6 us (0.15); the launches traced: 163 us -> 24.4 us
  local copies, waits for them, and re-layouts: 84.2 us -> 2.79 us
  blocking collectives: 44.5 us -> 0 us
  Pallas kernels: 0 us -> 20.9 us
  other arithmetic: 20.4 us -> 0 us
  matrix products: 6.68 us -> 0 us
  starting transfers between devices: 6.12 us -> 0 us
    gather x152 -> x0, local copies, waits for them, and re-layouts: 62.7 us -> none
    all_gather x1 -> x0, blocking collectives: 23.7 us -> none  [shards(): lax.all_gather(resolution.astype(jnp.bfloat16), 'exp', axis=2, tiled=True)]
    pallas_call x0 -> x1, Pallas kernels: none -> 20.9 us  [shards(): pl.pallas_call(functools.partial(kernel, n_e, n_c, skyc, comp), out_shape...]
    mul x11 -> x0, local copies, waits for them, and re-layouts: 13.6 us -> none  [band_model(): pieces[:, offset, None, :] * windows[:, :, offset:offset + length]]
    psum x1 -> x0, blocking collectives: 11.4 us -> none  [shards(): gram, target = lax.psum((gram, target), 'ccd')]
    all_to_all x1 -> x0, blocking collectives: 9.43 us -> none  [shards(): lax.all_to_all(residual[None], 'exp', split_axis=2, concat_axis=0, tiled=...]
    add x2 -> x0, other arithmetic: 6.48 us -> none  [the longest x1 6.47 us: band_model(): total + pieces[:, offset, None, :] * windows[:, :, offset:offset + length]]
    dot_general x7 -> x0, matrix products: 6.4 us -> none  [the longest x1 2.32 us: shards(): gram = jnp.einsum('fkw,flw->kl', weighted, model, precision=highest)]
  transfers between devices with their start and end apart: 2 -> 0, of which waited for: 0 -> 0; matrix products, arithmetic and copies ran while one was open for 54% -> 0% of each run, Pallas kernels for 0% -> 0%
where the time goes in v1:
time: 24.6 us; the launch traced here: 24.4 us
  Pallas kernels  20.9 us (85%)
  local copies, waits for them, and re-layouts  2.79 us (11%)
  between operations  0.7 us (3%)
    pallas_call x1, Pallas kernels, shards(): pl.pallas_call(functools.partial(kernel, n_e, n_c, skyc, comp), out_shape...  20.9 us
    unnamed x15, local copies, waits for them, and re-layouts  2.79 us

profile of v1, /device:TPU:0, one launch (start us, length us, event | category | flops | bytes accessed | tf_op | source)
XLA Modules:
  0.0 24.4 jit_solution(11418418924714706791)
XLA Ops:
  0.6 0.0 copy-start
  0.6 0.0 copy-start.1
  0.7 0.0 copy-start.2
  0.7 0.0 copy-start.3
  0.7 0.0 copy-start.4
  0.7 0.0 copy-start.5
  0.7 1.4 %copy.9.psf_hbm = bf16[2,100,2160]{2,1,0:T(8,128)(2,1)S(1)} copy(bf16[2,100,2160]{2,0,1:T(2,128)(2,1)} %param.8) | data formatting | bytes 1728000 | tf_op args[1]
  2.0 0.1 copy-done
  2.1 0.1 copy-done.1
  2.2 0.0 copy-done.2
  2.2 0.0 copy-done.3
  2.2 0.0 copy-done.4
  2.2 0.0 copy-done.5
  2.2 20.9 %extract.1 = (f32[50,8,64]{2,1,0:T(8,128)S(1)}, f32[50,64]{1,0:T(8,128)S(1)}) custom-call(bf16[4000,128]{1,0:T(8,128)(2,1)S(1)} %bitcast.5, bf16[2,100,2160]{2,1,0:T(8,128)(2,1)S(1)} %copy.9.psf_hbm, f32[11,50,64]{2,1,0:T(8,128)S(1)} %bitcast.6, f32[10,528]{1,0:T(8,128)S(1)} %copy-done.2, s32[1,50]{1,0:T(1,128)S(1)} %bitcast.8, s32[1,50]{1,0:T(1,128)S(1)} %bitcast.9, ...), custom_call_target="tpu_custom_call" | custom-call | tf_op jit(solution)/shard_map/extract/pallas_call | solution.py:383
  23.1 0.7 %copy.12 = f32[8,50,64]{2,0,1:T(8,128)} copy(f32[8,50,64]{2,0,1:T(8,128)S(1)} %bitcast.7) | data formatting | bytes 204800
  23.8 0.6 %copy.13 = f32[50,64]{1,0:T(8,128)} copy(f32[50,64]{1,0:T(8,128)S(1)} %get-tuple-element.9) | data formatting | bytes 25600
Async XLA Ops:
  0.6 1.5 %copy-start = (bf16[1,1000,4,128]{3,2,1,0:T(4,128)(2,1)S(1)}, bf16[1,1000,4,128]{3,2,1,0:T(4,128)(2,1)}, u32[]{:S(2)}) copy-start(bf16[1,1000,4,128]{3,2,1,0:T(4,128)(2,1)} %param.7) | copy-start | bytes 3072004
  0.6 1.5 %copy-start.1 = (f32[50,11,64]{2,0,1:T(8,128)S(1)}, f32[50,11,64]{2,0,1:T(8,128)}, u32[]{:S(2)}) copy-start(f32[50,11,64]{2,0,1:T(8,128)} %param.9) | copy-start | bytes 422404
  0.7 1.5 %copy-start.2 = (f32[10,528]{1,0:T(8,128)S(1)}, f32[10,528]{1,0:T(8,128)}, u32[]{:S(2)}) copy-start(f32[10,528]{1,0:T(8,128)} %basis_ref.1) | copy-start | bytes 63364
  0.7 1.5 %copy-start.3 = (s32[50]{0:T(128)S(1)}, s32[50]{0:T(128)}, u32[]{:S(2)}) copy-start(s32[50]{0:T(128)} %slot_s.1) | copy-start | bytes 604
  0.7 1.5 %copy-start.4 = (s32[50]{0:T(128)S(1)}, s32[50]{0:T(128)}, u32[]{:S(2)}) copy-start(s32[50]{0:T(128)} %shift_s.1) | copy-start | bytes 604
  0.7 1.5 %copy-start.5 = (s32[24]{0:T(128)S(1)}, s32[24]{0:T(128)}, u32[]{:S(2)}) copy-start(s32[24]{0:T(128)} %sky_s.1) | copy-start | bytes 292

commit v2 on v1

--- a/solution.py
+++ b/solution.py
@@ -18,7 +18,7 @@
 HALO = MARG * ROWS
 DEEP = SPAN * ROWS
 SLOTS = 64
-SKYROW = 56
+SKYROWS = 8
 MESH = pl.DeviceIdType.MESH
 
 
@@ -39,30 +39,25 @@
 
 def kernel(
     n_e, n_c, skyc, comp,
-    pix_hbm, psf_hbm, res_hbm, basis_ref, slot_row, shift_row, sky_s, slot_s, shift_s,
+    pix, psf, res, basis_ref, slot_row, shift_row, sky_s, slot_s, shift_s,
     out_ref, rms_ref,
-    xs, psf, res, res2, bpad, bsh, stage, skysend, skyrecv, skyfull, slots, fluxr,
+    before, after, res2, bpad, bsh, stage, skysend, skyrecv, skyfull, slots, fluxr,
     fsend, frecv, grecv, csend, crecv, croll, outs,
-    local_sem, halo_ssem, halo_rsem, sky_ssem, sky_rsem, f_ssem, f_rsem,
+    halo_ssem, halo_rsem, sky_ssem, sky_rsem, f_ssem, f_rsem,
     g_ssem, g_rsem, c_ssem, c_rsem,
 ):
     me = lax.axis_index("exp")
     mc = lax.axis_index("ccd")
     fc = res.shape[1]
     wl = res.shape[2]
-    own = pix_hbm.shape[0]
+    own = pix.shape[0]
+    inner = before.shape[0] - HALO
+    outer = after.shape[0] - HALO
     groups = LANES // wl
     tall = SLOTS // groups
     per = stage.shape[0]
     half = psf.shape[1]
     f32 = jnp.float32
-
-    get_res = pltpu.make_async_copy(res_hbm, res, local_sem.at[0])
-    get_psf = pltpu.make_async_copy(psf_hbm, psf, local_sem.at[1])
-    get_pix = pltpu.make_async_copy(pix_hbm, xs.at[pl.ds(HALO, own)], local_sem.at[2])
-    get_res.start()
-    get_psf.start()
-    get_pix.start()
 
     barrier = pltpu.get_barrier_semaphore()
     for d in range(1, n_e):
@@ -79,7 +74,6 @@
     stage[...] = jnp.zeros_like(stage)
     bpad[...] = jnp.zeros_like(bpad)
     bpad[0:comp, 0 : basis_ref.shape[1]] = basis_ref[...]
-    get_res.wait()
     for i in range(skyc):
         q, s = i // per, i % per
         for d in range(BAND):
@@ -90,8 +84,8 @@
 
     def to_left():
         return pltpu.make_async_remote_copy(
-            src_ref=pix_hbm.at[pl.ds(0, HALO)],
-            dst_ref=xs.at[pl.ds(HALO + own, HALO)],
+            src_ref=pix.at[pl.ds(0, HALO)],
+            dst_ref=after.at[pl.ds(outer, HALO)],
             send_sem=halo_ssem.at[0],
             recv_sem=halo_rsem.at[0],
             device_id={"ccd": lax.rem(mc + n_c - 1, n_c)},
@@ -100,8 +94,8 @@
 
     def to_right():
         return pltpu.make_async_remote_copy(
-            src_ref=pix_hbm.at[pl.ds(own - HALO, HALO)],
-            dst_ref=xs.at[pl.ds(0, HALO)],
+            src_ref=pix.at[pl.ds(own - HALO, HALO)],
+            dst_ref=before.at[pl.ds(0, HALO)],
             send_sem=halo_ssem.at[1],
             recv_sem=halo_rsem.at[1],
             device_id={"ccd": lax.rem(mc + 1, n_c)},
@@ -116,13 +110,16 @@
     def _():
         to_right().start()
 
+    before[HALO:, :] = pix[0:inner, :]
+    after[0:outer, :] = pix[own - outer :, :]
+
     @pl.when(mc == 0)
     def _():
-        xs[0:HALO, :] = jnp.zeros((HALO, LANES), xs.dtype)
+        before[0:HALO, :] = jnp.zeros((HALO, LANES), before.dtype)
 
     @pl.when(mc == n_c - 1)
     def _():
-        xs[HALO + own :, :] = jnp.zeros((HALO, LANES), xs.dtype)
+        after[outer:, :] = jnp.zeros((HALO, LANES), after.dtype)
 
     def exchange(axis, size, mine, source, landing, ssem, rsem):
         sends, receives = [], []
@@ -159,23 +156,25 @@
     slot = column_of(slot_row[...], SLOTS) - mc * fc
     place = lax.broadcasted_iota(jnp.int32, (SLOTS, 1), 0)
     slot = jnp.where(place < fc, slot, -1000)
+    sky_place = lax.broadcasted_iota(jnp.int32, (SKYROWS, 1), 0)
+    sky_slot = jnp.full((SKYROWS, 1), -1000, jnp.int32)
     for i in range(skyc):
-        slot = jnp.where(place == SKYROW + i, slot_s[sky[i]] - mc * fc, slot)
+        sky_slot = jnp.where(sky_place == i, slot_s[sky[i]] - mc * fc, sky_slot)
     gap = slots.shape[0] // 2 - half
-    first = slot * ROWS + jnp.where(slot * ROWS >= half, gap, 0)
-    lane = lax.broadcasted_iota(jnp.int32, (SLOTS, slots.shape[0]), 1)
-    pick = jnp.concatenate(
-        [jnp.where(lane == first + r, 1.0, 0.0) for r in range(ROWS)], axis=0
-    ).astype(jnp.bfloat16)
+
+    def picker(rows):
+        first = rows * ROWS + jnp.where(rows * ROWS >= half, gap, 0)
+        lane = lax.broadcasted_iota(jnp.int32, (rows.shape[0], slots.shape[0]), 1)
+        return jnp.concatenate(
+            [jnp.where(lane == first + r, 1.0, 0.0) for r in range(ROWS)], axis=0
+        ).astype(jnp.bfloat16)
+
+    sky_pick, pick = picker(sky_slot), picker(slot)
 
     slots[...] = jnp.zeros_like(slots)
-    get_psf.wait()
-    get_pix.wait()
-
-    def partial(block, lower, upper):
+
+    def partial(block, lower, upper, window):
         weights = psf[block, :, lower:upper]
-        start = block * BPIX * ROWS
-        window = xs[start + lower : start + upper, :]
         wide_w = weights.astype(f32)
         wide_x = window.astype(f32)
         squares = (wide_w * wide_w).astype(jnp.bfloat16)
@@ -187,10 +186,14 @@
     blocks = psf.shape[0]
     cuts = []
     for b in range(blocks):
-        lower = LANES if b == 0 else 0
-        upper = (DEEP - HALO) // LANES * LANES if b == blocks - 1 else DEEP
+        lower = before.shape[0] if b == 0 else 0
+        upper = DEEP - after.shape[0] if b == blocks - 1 else DEEP
         cuts.append((lower, upper))
-    main = [partial(b, *cuts[b]) for b in range(blocks)]
+    main = []
+    for b in range(blocks):
+        start = b * BPIX * ROWS - HALO
+        lower, upper = cuts[b]
+        main.append(partial(b, lower, upper, pix[start + lower : start + upper, :]))
 
     @pl.when(mc < n_c - 1)
     def _():
@@ -205,30 +208,22 @@
         flux, var = main[b]
         lower, upper = cuts[b]
         if lower > 0:
-            more = partial(b, 0, lower)
+            more = partial(b, 0, lower, before[...])
             flux, var = flux + more[0], var + more[1]
         if upper < DEEP:
-            more = partial(b, upper, DEEP)
+            more = partial(b, upper, DEEP, after[...])
             flux, var = flux + more[0], var + more[1]
         slots[b * pitch : b * pitch + half, 0:LANES] = flux
         slots[b * pitch : b * pitch + half, LANES:] = var
 
-    high, mid, low = pieces_of(slots[...])
+    pieces = pieces_of(slots[...])
     dot = functools.partial(jnp.dot, preferred_element_type=f32)
-    chosen = dot(pick, high) + (dot(pick, mid) + dot(pick, low))
-    fluxr[...] = chosen
-
-    for j in range(n_e):
-        r, off = j * wl // LANES, j * wl % LANES
-        for q in range(groups):
-            rows = pl.ds(r * SLOTS + q * tall, tall)
-            fsend[j, :, q * wl : (q + 1) * wl] = fluxr[rows, off : off + wl]
-    f_out, f_in = exchange(
-        "exp", n_e, me, lambda there: fsend.at[there], frecv, f_ssem, f_rsem
-    )
-    for copy in f_out:
-        copy.start()
-    frecv[me] = fsend[me]
+
+    def chosen(rows, lower, upper):
+        parts = [dot(rows, x[:, lower:upper]) for x in pieces]
+        return parts[0] + (parts[1] + parts[2])
+
+    sky_rows = chosen(sky_pick, 0, 2 * LANES)
 
     for copy in sky_in:
         copy.wait_recv()
@@ -244,9 +239,9 @@
         model = jnp.zeros((16, wide), f32)
         for d in range(BAND):
             model = model + skyfull[i, d : d + 1, :] * bsh[offset + d]
-        rows = [r * SLOTS + SKYROW + i for r in range(ROWS)]
-        flux = jnp.concatenate([fluxr[x : x + 1, 0:LANES] for x in rows], axis=1)
-        var = jnp.concatenate([fluxr[x : x + 1, LANES:] for x in rows], axis=1)
+        rows = [r * SKYROWS + i for r in range(ROWS)]
+        flux = jnp.concatenate([sky_rows[x : x + 1, 0:LANES] for x in rows], axis=1)
+        var = jnp.concatenate([sky_rows[x : x + 1, LANES:] for x in rows], axis=1)
         full = jnp.where(sub == comp, flux, model)
         weighted = full * (1.0 / var)
         for col in range(comp + 1):
@@ -265,6 +260,20 @@
     for copy in g_out:
         copy.start()
 
+    fluxr[...] = chosen(pick, 0, LANES)
+
+    for j in range(n_e):
+        r, off = j * wl // LANES, j * wl % LANES
+        for q in range(groups):
+            rows = pl.ds(r * SLOTS + q * tall, tall)
+            fsend[j, :, q * wl : (q + 1) * wl] = fluxr[rows, off : off + wl]
+    f_out, f_in = exchange(
+        "exp", n_e, me, lambda there: fsend.at[there], frecv, f_ssem, f_rsem
+    )
+    for copy in f_out:
+        copy.start()
+    frecv[me] = fsend[me]
+
     planes = [res[d] for d in range(BAND)]
     shift = column_of(shift_row[...], fc) + SHIFT
     for step in (1, 2, 4):
@@ -273,8 +282,8 @@
         moved = []
         for e in range(length):
             here = planes[e] if e < len(planes) else jnp.zeros((fc, wl), f32)
-            before = planes[e - step] if e >= step else jnp.zeros((fc, wl), f32)
-            moved.append(jnp.where(take, before, here))
+            prior = planes[e - step] if e >= step else jnp.zeros((fc, wl), f32)
+            moved.append(jnp.where(take, prior, here))
         planes = moved
     for e in range(TAPS):
         res2[e] = planes[e]
@@ -339,6 +348,15 @@
         copy.wait_send()
 
 
+def deliver(cube_ref, rms_ref, cube_out, rms_out, sem):
+    first = pltpu.make_async_copy(cube_ref, cube_out, sem.at[0])
+    second = pltpu.make_async_copy(rms_ref, rms_out, sem.at[1])
+    first.start()
+    second.start()
+    first.wait()
+    second.wait()
+
+
 def shards(n_e, n_c, pixels, psf_proj, resolution, basis, sky_fibres, fibre_slot, band_shift):
     fc, band, wl = resolution.shape
     comp, ext = basis.shape
@@ -355,9 +373,8 @@
     smem = pl.BlockSpec(memory_space=pltpu.SMEM)
     dma = pltpu.SemaphoreType.DMA
     scratch = [
-        pltpu.VMEM((own + 2 * HALO, LANES), bf16),
-        pltpu.VMEM(psf_proj.shape, bf16),
-        pltpu.VMEM((band, fc, wl), f32),
+        pltpu.VMEM((LANES, LANES), bf16),
+        pltpu.VMEM((DEEP - (DEEP - HALO) // LANES * LANES, LANES), bf16),
         pltpu.VMEM((TAPS, fc, wl), f32),
         pltpu.VMEM((16, wave + LANES), f32),
         pltpu.VMEM((TAPS, 16, wave), f32),
@@ -366,7 +383,7 @@
         pltpu.VMEM((n_e, per, 16, LANES), bf16),
         pltpu.VMEM((skyc, 16, wave), f32),
         pltpu.VMEM((2 * pitch, 2 * LANES), f32),
-        pltpu.VMEM((ROWS * SLOTS, 2 * LANES), f32),
+        pltpu.VMEM((ROWS * SLOTS, LANES), f32),
         pltpu.VMEM((n_e, SLOTS // groups, LANES), f32),
         pltpu.VMEM((n_e, SLOTS // groups, LANES), f32),
         pltpu.VMEM((n_c, 16, LANES), f32),
@@ -374,7 +391,6 @@
         pltpu.VMEM((n_e, 1, LANES), f32),
         pltpu.VMEM((TAPS, n_e, LANES), f32),
         pltpu.VMEM((n_e, fc, wl), f32),
-        dma((3,)),
         dma((2,)),
         dma((2,)),
     ]
@@ -386,7 +402,7 @@
             jax.ShapeDtypeStruct((fc, n_e, wl), f32),
             jax.ShapeDtypeStruct((fc, wl), f32),
         ),
-        in_specs=[anywhere, anywhere, anywhere, vmem, vmem, vmem, smem, smem, smem],
+        in_specs=[vmem, vmem, vmem, vmem, vmem, vmem, smem, smem, smem],
         out_specs=(vmem, vmem),
         scratch_shapes=scratch,
         compiler_params=pltpu.CompilerParams(
@@ -404,6 +420,17 @@
         fibre_slot,
         band_shift,
     )
+    cube, rms = pl.pallas_call(
+        deliver,
+        out_shape=(
+            jax.ShapeDtypeStruct(cube.shape, f32),
+            jax.ShapeDtypeStruct(rms.shape, f32),
+        ),
+        in_specs=[anywhere, anywhere],
+        out_specs=(anywhere, anywhere),
+        scratch_shapes=[dma((2,))],
+        name="deliver",
+    )(cube, rms)
     return jnp.swapaxes(cube, 0, 1), rms
 
 

time: 24.6 us -> 31.9 us (1.30)
  Pallas kernels: 20.9 us -> 28.3 us
    pallas_call x0 -> x1, Pallas kernels: none -> 8.1 us  [shards(): pl.pallas_call(deliver, out_shape=(jax.ShapeDtypeStruct(cube.shape, f32),...]
    pallas_call x1, Pallas kernels: 20.9 us -> 20.2 us  [shards(): pl.pallas_call(functools.partial(kernel, n_e, n_c, skyc, comp), out_shape...]
    unnamed x15 -> x17, local copies, waits for them, and re-layouts: 2.79 us -> 2.77 us
where the time goes in v2:
time: 31.9 us; the launch traced here: 31.8 us
  Pallas kernels  28.3 us (89%)
  local copies, waits for them, and re-layouts  2.77 us (9%)
  between operations  0.71 us (2%)
    pallas_call x1, Pallas kernels, shards(): pl.pallas_call(functools.partial(kernel, n_e, n_c, skyc, comp), out_shape...  20.2 us
    pallas_call x1, Pallas kernels, shards(): pl.pallas_call(deliver, out_shape=(jax.ShapeDtypeStruct(cube.shape, f32),...  8.1 us
    unnamed x17, local copies, waits for them, and re-layouts  2.77 us

profile of v2, /device:TPU:0, one launch (start us, length us, event | category | flops | bytes accessed | tf_op | source)
XLA Modules:
  0.0 31.8 jit_solution(8080060908570893572)
XLA Ops:
  0.6 0.0 copy-start
  0.6 0.0 copy-start.1
  0.7 0.0 copy-start.3
  0.7 0.0 copy-start.5
  0.7 0.0 copy-start.6
  0.7 0.0 copy-start.7
  0.7 1.4 %copy.9.psf = bf16[2,100,2160]{2,1,0:T(8,128)(2,1)S(1)} copy(bf16[2,100,2160]{2,0,1:T(2,128)(2,1)} %param.8) | data formatting | bytes 1728000 | tf_op args[1]
  2.0 0.1 copy-done
  2.1 0.1 copy-done.1
  2.2 0.0 copy-done.3
  2.2 0.0 copy-done.5
  2.2 0.0 copy-done.6
  2.2 0.0 copy-done.7
  2.2 20.2 %extract.1 = (f32[50,8,64]{2,1,0:T(8,128)S(1)}, f32[50,64]{1,0:T(8,128)S(1)}) custom-call(bf16[4000,128]{1,0:T(8,128)(2,1)S(1)} %bitcast.5, bf16[2,100,2160]{2,1,0:T(8,128)(2,1)S(1)} %copy.9.psf, f32[11,50,64]{2,1,0:T(8,128)S(1)} %bitcast.6, f32[10,528]{1,0:T(8,128)S(1)} %copy-done.3, s32[1,50]{1,0:T(1,128)S(1)} %bitcast.7, s32[1,50]{1,0:T(1,128)S(1)} %bitcast.8, ...), custom_call_target="tpu_custom_call" | custom-call | tf_op jit(solution)/shard_map/extract/pallas_call | solution.py:399
  22.4 0.0 copy-start.2
  22.4 0.7 %copy-done.2 = f32[50,8,64]{2,1,0:T(8,128)} copy-done((f32[50,8,64]{2,1,0:T(8,128)}, f32[50,8,64]{2,1,0:T(8,128)S(1)}, u32[]{:S(2)}) %copy-start.2) | copy-done | bytes 102424
  23.0 0.0 copy-start.4
  23.1 0.6 %copy-done.4 = f32[50,64]{1,0:T(8,128)} copy-done((f32[50,64]{1,0:T(8,128)}, f32[50,64]{1,0:T(8,128)S(1)}, u32[]{:S(2)}) %copy-start.4) | copy-done | bytes 12824
  23.7 8.1 %deliver.1 = (f32[50,8,64]{2,1,0:T(8,128)}, f32[50,64]{1,0:T(8,128)}) custom-call(f32[50,8,64]{2,1,0:T(8,128)} %copy-done.2, f32[50,64]{1,0:T(8,128)} %copy-done.4), custom_call_target="tpu_custom_call" | custom-call | tf_op jit(solution)/shard_map/deliver/pallas_call | solution.py:423
Async XLA Ops:
  0.6 1.5 %copy-start = (bf16[1,1000,4,128]{3,2,1,0:T(4,128)(2,1)S(1)}, bf16[1,1000,4,128]{3,2,1,0:T(4,128)(2,1)}, u32[]{:S(2)}) copy-start(bf16[1,1000,4,128]{3,2,1,0:T(4,128)(2,1)} %param.7) | copy-start | bytes 3072004
  0.6 1.5 %copy-start.1 = (f32[50,11,64]{2,0,1:T(8,128)S(1)}, f32[50,11,64]{2,0,1:T(8,128)}, u32[]{:S(2)}) copy-start(f32[50,11,64]{2,0,1:T(8,128)} %param.9) | copy-start | bytes 422404
  0.7 1.5 %copy-start.3 = (f32[10,528]{1,0:T(8,128)S(1)}, f32[10,528]{1,0:T(8,128)}, u32[]{:S(2)}) copy-start(f32[10,528]{1,0:T(8,128)} %basis_ref.1) | copy-start | bytes 63364
  0.7 1.5 %copy-start.5 = (s32[50]{0:T(128)S(1)}, s32[50]{0:T(128)}, u32[]{:S(2)}) copy-start(s32[50]{0:T(128)} %slot_s.1) | copy-start | bytes 604
  0.7 1.5 %copy-start.6 = (s32[50]{0:T(128)S(1)}, s32[50]{0:T(128)}, u32[]{:S(2)}) copy-start(s32[50]{0:T(128)} %shift_s.1) | copy-start | bytes 604
  0.7 1.5 %copy-start.7 = (s32[24]{0:T(128)S(1)}, s32[24]{0:T(128)}, u32[]{:S(2)}) copy-start(s32[24]{0:T(128)} %sky_s.1) | copy-start | bytes 292
  22.4 0.7 %copy-start.2 = (f32[50,8,64]{2,1,0:T(8,128)}, f32[50,8,64]{2,1,0:T(8,128)S(1)}, u32[]{:S(2)}) copy-start(f32[50,8,64]{2,1,0:T(8,128)S(1)} %get-tuple-element.6.cube_ref) | copy-start | bytes 307204
  23.0 0.6 %copy-start.4 = (f32[50,64]{1,0:T(8,128)}, f32[50,64]{1,0:T(8,128)S(1)}, u32[]{:S(2)}) copy-start(f32[50,64]{1,0:T(8,128)S(1)} %get-tuple-element.7.rms_ref) | copy-start | bytes 38404

commit v3 on v2

--- a/solution.py
+++ b/solution.py
@@ -224,6 +224,20 @@
         return parts[0] + (parts[1] + parts[2])
 
     sky_rows = chosen(sky_pick, 0, 2 * LANES)
+
+    fluxr[...] = chosen(pick, 0, LANES)
+
+    for j in range(n_e):
+        r, off = j * wl // LANES, j * wl % LANES
+        for q in range(groups):
+            rows = pl.ds(r * SLOTS + q * tall, tall)
+            fsend[j, :, q * wl : (q + 1) * wl] = fluxr[rows, off : off + wl]
+    f_out, f_in = exchange(
+        "exp", n_e, me, lambda there: fsend.at[there], frecv, f_ssem, f_rsem
+    )
+    for copy in f_out:
+        copy.start()
+    frecv[me] = fsend[me]
 
     for copy in sky_in:
         copy.wait_recv()
@@ -259,20 +273,6 @@
     )
     for copy in g_out:
         copy.start()
-
-    fluxr[...] = chosen(pick, 0, LANES)
-
-    for j in range(n_e):
-        r, off = j * wl // LANES, j * wl % LANES
-        for q in range(groups):
-            rows = pl.ds(r * SLOTS + q * tall, tall)
-            fsend[j, :, q * wl : (q + 1) * wl] = fluxr[rows, off : off + wl]
-    f_out, f_in = exchange(
-        "exp", n_e, me, lambda there: fsend.at[there], frecv, f_ssem, f_rsem
-    )
-    for copy in f_out:
-        copy.start()
-    frecv[me] = fsend[me]
 
     planes = [res[d] for d in range(BAND)]
     shift = column_of(shift_row[...], fc) + SHIFT
@@ -426,7 +426,7 @@
             jax.ShapeDtypeStruct(cube.shape, f32),
             jax.ShapeDtypeStruct(rms.shape, f32),
         ),
-        in_specs=[anywhere, anywhere],
+        in_specs=[vmem, vmem],
         out_specs=(anywhere, anywhere),
         scratch_shapes=[dma((2,))],
         name="deliver",

time: 31.9 us -> 25.5 us (0.80)
  Pallas kernels: 28.3 us -> 21.9 us
    pallas_call x1, Pallas kernels: 8.1 us -> 1.63 us  [shards(): pl.pallas_call(deliver, out_shape=(jax.ShapeDtypeStruct(cube.shape, f32),...]
where the time goes in v3:
time: 25.5 us; the launch traced here: 25.3 us
  Pallas kernels  21.9 us (86%)
  local copies, waits for them, and re-layouts  2.77 us (11%)
  between operations  0.71 us (3%)
    pallas_call x1, Pallas kernels, shards(): pl.pallas_call(functools.partial(kernel, n_e, n_c, skyc, comp), out_shape...  20.2 us
    unnamed x17, local copies, waits for them, and re-layouts  2.77 us
    pallas_call x1, Pallas kernels, shards(): pl.pallas_call(deliver, out_shape=(jax.ShapeDtypeStruct(cube.shape, f32),...  1.63 us

profile of v3, /device:TPU:0, one launch (start us, length us, event | category | flops | bytes accessed | tf_op | source)
XLA Modules:
  0.0 25.3 jit_solution(871228670774364585)
XLA Ops:
  0.6 0.0 copy-start
  0.6 0.0 copy-start.1
  0.7 0.0 copy-start.3
  0.7 0.0 copy-start.5
  0.7 0.0 copy-start.6
  0.7 0.0 copy-start.7
  0.7 1.4 %copy.9.psf = bf16[2,100,2160]{2,1,0:T(8,128)(2,1)S(1)} copy(bf16[2,100,2160]{2,0,1:T(2,128)(2,1)} %param.8) | data formatting | bytes 1728000 | tf_op args[1]
  2.0 0.1 copy-done
  2.1 0.1 copy-done.1
  2.2 0.0 copy-done.3
  2.2 0.0 copy-done.5
  2.2 0.0 copy-done.6
  2.2 0.0 copy-done.7
  2.2 20.2 %extract.1 = (f32[50,8,64]{2,1,0:T(8,128)S(1)}, f32[50,64]{1,0:T(8,128)S(1)}) custom-call(bf16[4000,128]{1,0:T(8,128)(2,1)S(1)} %bitcast.5, bf16[2,100,2160]{2,1,0:T(8,128)(2,1)S(1)} %copy.9.psf, f32[11,50,64]{2,1,0:T(8,128)S(1)} %bitcast.6, f32[10,528]{1,0:T(8,128)S(1)} %copy-done.3, s32[1,50]{1,0:T(1,128)S(1)} %bitcast.7, s32[1,50]{1,0:T(1,128)S(1)} %bitcast.8, ...), custom_call_target="tpu_custom_call" | custom-call | tf_op jit(solution)/shard_map/extract/pallas_call | solution.py:399
  22.4 0.0 copy-start.2
  22.4 0.7 %copy-done.2 = f32[50,8,64]{2,1,0:T(8,128)} copy-done((f32[50,8,64]{2,1,0:T(8,128)}, f32[50,8,64]{2,1,0:T(8,128)S(1)}, u32[]{:S(2)}) %copy-start.2) | copy-done | bytes 102424
  23.1 0.0 copy-start.4
  23.1 0.6 %copy-done.4 = f32[50,64]{1,0:T(8,128)} copy-done((f32[50,64]{1,0:T(8,128)}, f32[50,64]{1,0:T(8,128)S(1)}, u32[]{:S(2)}) %copy-start.4) | copy-done | bytes 12824
  23.7 1.6 %deliver.1 = (f32[50,8,64]{2,1,0:T(8,128)}, f32[50,64]{1,0:T(8,128)}) custom-call(f32[50,8,64]{2,1,0:T(8,128)} %copy-done.2, f32[50,64]{1,0:T(8,128)} %copy-done.4), custom_call_target="tpu_custom_call" | custom-call | tf_op jit(solution)/shard_map/deliver/pallas_call | solution.py:423
Async XLA Ops:
  0.6 1.5 %copy-start = (bf16[1,1000,4,128]{3,2,1,0:T(4,128)(2,1)S(1)}, bf16[1,1000,4,128]{3,2,1,0:T(4,128)(2,1)}, u32[]{:S(2)}) copy-start(bf16[1,1000,4,128]{3,2,1,0:T(4,128)(2,1)} %param.7) | copy-start | bytes 3072004
  0.6 1.5 %copy-start.1 = (f32[50,11,64]{2,0,1:T(8,128)S(1)}, f32[50,11,64]{2,0,1:T(8,128)}, u32[]{:S(2)}) copy-start(f32[50,11,64]{2,0,1:T(8,128)} %param.9) | copy-start | bytes 422404
  0.7 1.5 %copy-start.3 = (f32[10,528]{1,0:T(8,128)S(1)}, f32[10,528]{1,0:T(8,128)}, u32[]{:S(2)}) copy-start(f32[10,528]{1,0:T(8,128)} %basis_ref.1) | copy-start | bytes 63364
  0.7 1.5 %copy-start.5 = (s32[50]{0:T(128)S(1)}, s32[50]{0:T(128)}, u32[]{:S(2)}) copy-start(s32[50]{0:T(128)} %slot_s.1) | copy-start | bytes 604
  0.7 1.5 %copy-start.6 = (s32[50]{0:T(128)S(1)}, s32[50]{0:T(128)}, u32[]{:S(2)}) copy-start(s32[50]{0:T(128)} %shift_s.1) | copy-start | bytes 604
  0.7 1.5 %copy-start.7 = (s32[24]{0:T(128)S(1)}, s32[24]{0:T(128)}, u32[]{:S(2)}) copy-start(s32[24]{0:T(128)} %sky_s.1) | copy-start | bytes 292
  22.4 0.7 %copy-start.2 = (f32[50,8,64]{2,1,0:T(8,128)}, f32[50,8,64]{2,1,0:T(8,128)S(1)}, u32[]{:S(2)}) copy-start(f32[50,8,64]{2,1,0:T(8,128)S(1)} %get-tuple-element.6.cube_ref) | copy-start | bytes 307204
  23.1 0.6 %copy-start.4 = (f32[50,64]{1,0:T(8,128)}, f32[50,64]{1,0:T(8,128)S(1)}, u32[]{:S(2)}) copy-start(f32[50,64]{1,0:T(8,128)S(1)} %get-tuple-element.7.rms_ref) | copy-start | bytes 38404

commit v4 on v3

--- a/solution.py
+++ b/solution.py
@@ -348,15 +348,6 @@
         copy.wait_send()
 
 
-def deliver(cube_ref, rms_ref, cube_out, rms_out, sem):
-    first = pltpu.make_async_copy(cube_ref, cube_out, sem.at[0])
-    second = pltpu.make_async_copy(rms_ref, rms_out, sem.at[1])
-    first.start()
-    second.start()
-    first.wait()
-    second.wait()
-
-
 def shards(n_e, n_c, pixels, psf_proj, resolution, basis, sky_fibres, fibre_slot, band_shift):
     fc, band, wl = resolution.shape
     comp, ext = basis.shape
@@ -368,7 +359,6 @@
     half = psf_proj.shape[1]
     pitch = -(-half // 8) * 8
     f32, bf16 = jnp.float32, jnp.bfloat16
-    anywhere = pl.BlockSpec(memory_space=pl.ANY)
     vmem = pl.BlockSpec(memory_space=pltpu.VMEM)
     smem = pl.BlockSpec(memory_space=pltpu.SMEM)
     dma = pltpu.SemaphoreType.DMA
@@ -420,17 +410,6 @@
         fibre_slot,
         band_shift,
     )
-    cube, rms = pl.pallas_call(
-        deliver,
-        out_shape=(
-            jax.ShapeDtypeStruct(cube.shape, f32),
-            jax.ShapeDtypeStruct(rms.shape, f32),
-        ),
-        in_specs=[vmem, vmem],
-        out_specs=(anywhere, anywhere),
-        scratch_shapes=[dma((2,))],
-        name="deliver",
-    )(cube, rms)
     return jnp.swapaxes(cube, 0, 1), rms
 
 

time: 25.5 us -> 23.9 us (0.937)
  Pallas kernels: 21.9 us -> 20.2 us
    pallas_call x1 -> x0, Pallas kernels: 1.63 us -> none  [shards(): pl.pallas_call(deliver, out_shape=(jax.ShapeDtypeStruct(cube.shape, f32),...]
    unnamed x17 -> x15, local copies, waits for them, and re-layouts: 2.77 us -> 2.79 us
where the time goes in v4:
time: 23.9 us; the launch traced here: 23.7 us
  Pallas kernels  20.2 us (85%)
  local copies, waits for them, and re-layouts  2.79 us (12%)
  between operations  0.7 us (3%)
    pallas_call x1, Pallas kernels, shards(): pl.pallas_call(functools.partial(kernel, n_e, n_c, skyc, comp), out_shape...  20.2 us
    unnamed x15, local copies, waits for them, and re-layouts  2.79 us

profile of v4, /device:TPU:0, one launch (start us, length us, event | category | flops | bytes accessed | tf_op | source)
XLA Modules:
  0.0 23.7 jit_solution(16332555726778057983)
XLA Ops:
  0.6 0.0 copy-start
  0.6 0.0 copy-start.1
  0.7 0.0 copy-start.2
  0.7 0.0 copy-start.3
  0.7 0.0 copy-start.4
  0.7 0.0 copy-start.5
  0.7 1.4 %copy.9.psf = bf16[2,100,2160]{2,1,0:T(8,128)(2,1)S(1)} copy(bf16[2,100,2160]{2,0,1:T(2,128)(2,1)} %param.8) | data formatting | bytes 1728000 | tf_op args[1]
  2.0 0.1 copy-done
  2.1 0.1 copy-done.1
  2.2 0.0 copy-done.2
  2.2 0.0 copy-done.3
  2.2 0.0 copy-done.4
  2.2 0.0 copy-done.5
  2.2 20.2 %extract.1 = (f32[50,8,64]{2,1,0:T(8,128)S(1)}, f32[50,64]{1,0:T(8,128)S(1)}) custom-call(bf16[4000,128]{1,0:T(8,128)(2,1)S(1)} %bitcast.5, bf16[2,100,2160]{2,1,0:T(8,128)(2,1)S(1)} %copy.9.psf, f32[11,50,64]{2,1,0:T(8,128)S(1)} %bitcast.6, f32[10,528]{1,0:T(8,128)S(1)} %copy-done.2, s32[1,50]{1,0:T(1,128)S(1)} %bitcast.8, s32[1,50]{1,0:T(1,128)S(1)} %bitcast.9, ...), custom_call_target="tpu_custom_call" | custom-call | tf_op jit(solution)/shard_map/extract/pallas_call | solution.py:389
  22.4 0.7 %copy.12 = f32[8,50,64]{2,0,1:T(8,128)} copy(f32[8,50,64]{2,0,1:T(8,128)S(1)} %bitcast.7) | data formatting | bytes 204800
  23.1 0.6 %copy.13 = f32[50,64]{1,0:T(8,128)} copy(f32[50,64]{1,0:T(8,128)S(1)} %get-tuple-element.9) | data formatting | bytes 25600
Async XLA Ops:
  0.6 1.5 %copy-start = (bf16[1,1000,4,128]{3,2,1,0:T(4,128)(2,1)S(1)}, bf16[1,1000,4,128]{3,2,1,0:T(4,128)(2,1)}, u32[]{:S(2)}) copy-start(bf16[1,1000,4,128]{3,2,1,0:T(4,128)(2,1)} %param.7) | copy-start | bytes 3072004
  0.6 1.5 %copy-start.1 = (f32[50,11,64]{2,0,1:T(8,128)S(1)}, f32[50,11,64]{2,0,1:T(8,128)}, u32[]{:S(2)}) copy-start(f32[50,11,64]{2,0,1:T(8,128)} %param.9) | copy-start | bytes 422404
  0.7 1.5 %copy-start.2 = (f32[10,528]{1,0:T(8,128)S(1)}, f32[10,528]{1,0:T(8,128)}, u32[]{:S(2)}) copy-start(f32[10,528]{1,0:T(8,128)} %basis_ref.1) | copy-start | bytes 63364
  0.7 1.5 %copy-start.3 = (s32[50]{0:T(128)S(1)}, s32[50]{0:T(128)}, u32[]{:S(2)}) copy-start(s32[50]{0:T(128)} %slot_s.1) | copy-start | bytes 604
  0.7 1.5 %copy-start.4 = (s32[50]{0:T(128)S(1)}, s32[50]{0:T(128)}, u32[]{:S(2)}) copy-start(s32[50]{0:T(128)} %shift_s.1) | copy-start | bytes 604
  0.7 1.5 %copy-start.5 = (s32[24]{0:T(128)S(1)}, s32[24]{0:T(128)}, u32[]{:S(2)}) copy-start(s32[24]{0:T(128)} %sky_s.1) | copy-start | bytes 292

commit v5 on v2

--- a/solution.py
+++ b/solution.py
@@ -348,15 +348,6 @@
         copy.wait_send()
 
 
-def deliver(cube_ref, rms_ref, cube_out, rms_out, sem):
-    first = pltpu.make_async_copy(cube_ref, cube_out, sem.at[0])
-    second = pltpu.make_async_copy(rms_ref, rms_out, sem.at[1])
-    first.start()
-    second.start()
-    first.wait()
-    second.wait()
-
-
 def shards(n_e, n_c, pixels, psf_proj, resolution, basis, sky_fibres, fibre_slot, band_shift):
     fc, band, wl = resolution.shape
     comp, ext = basis.shape
@@ -368,7 +359,6 @@
     half = psf_proj.shape[1]
     pitch = -(-half // 8) * 8
     f32, bf16 = jnp.float32, jnp.bfloat16
-    anywhere = pl.BlockSpec(memory_space=pl.ANY)
     vmem = pl.BlockSpec(memory_space=pltpu.VMEM)
     smem = pl.BlockSpec(memory_space=pltpu.SMEM)
     dma = pltpu.SemaphoreType.DMA
@@ -420,17 +410,6 @@
         fibre_slot,
         band_shift,
     )
-    cube, rms = pl.pallas_call(
-        deliver,
-        out_shape=(
-            jax.ShapeDtypeStruct(cube.shape, f32),
-            jax.ShapeDtypeStruct(rms.shape, f32),
-        ),
-        in_specs=[anywhere, anywhere],
-        out_specs=(anywhere, anywhere),
-        scratch_shapes=[dma((2,))],
-        name="deliver",
-    )(cube, rms)
     return jnp.swapaxes(cube, 0, 1), rms
 
 

time: 31.9 us -> 23.8 us (0.75)
  Pallas kernels: 28.3 us -> 20.2 us
    pallas_call x1 -> x0, Pallas kernels: 8.1 us -> none  [shards(): pl.pallas_call(deliver, out_shape=(jax.ShapeDtypeStruct(cube.shape, f32),...]
    unnamed x17 -> x15, local copies, waits for them, and re-layouts: 2.77 us -> 2.79 us
where the time goes in v5:
time: 23.8 us; the launch traced here: 23.7 us
  Pallas kernels  20.2 us (85%)
  local copies, waits for them, and re-layouts  2.79 us (12%)
  between operations  0.7 us (3%)
    pallas_call x1, Pallas kernels, shards(): pl.pallas_call(functools.partial(kernel, n_e, n_c, skyc, comp), out_shape...  20.2 us
    unnamed x15, local copies, waits for them, and re-layouts  2.79 us

profile of v5, /device:TPU:0, one launch (start us, length us, event | category | flops | bytes accessed | tf_op | source)
XLA Modules:
  0.0 23.7 jit_solution(10700957914002006423)
XLA Ops:
  0.6 0.0 copy-start
  0.6 0.0 copy-start.1
  0.7 0.0 copy-start.2
  0.7 0.0 copy-start.3
  0.7 0.0 copy-start.4
  0.7 0.0 copy-start.5
  0.7 1.4 %copy.9.psf = bf16[2,100,2160]{2,1,0:T(8,128)(2,1)S(1)} copy(bf16[2,100,2160]{2,0,1:T(2,128)(2,1)} %param.8) | data formatting | bytes 1728000 | tf_op args[1]
  2.0 0.1 copy-done
  2.1 0.1 copy-done.1
  2.2 0.0 copy-done.2
  2.2 0.0 copy-done.3
  2.2 0.0 copy-done.4
  2.2 0.0 copy-done.5
  2.2 20.2 %extract.1 = (f32[50,8,64]{2,1,0:T(8,128)S(1)}, f32[50,64]{1,0:T(8,128)S(1)}) custom-call(bf16[4000,128]{1,0:T(8,128)(2,1)S(1)} %bitcast.5, bf16[2,100,2160]{2,1,0:T(8,128)(2,1)S(1)} %copy.9.psf, f32[11,50,64]{2,1,0:T(8,128)S(1)} %bitcast.6, f32[10,528]{1,0:T(8,128)S(1)} %copy-done.2, s32[1,50]{1,0:T(1,128)S(1)} %bitcast.8, s32[1,50]{1,0:T(1,128)S(1)} %bitcast.9, ...), custom_call_target="tpu_custom_call" | custom-call | tf_op jit(solution)/shard_map/extract/pallas_call | solution.py:389
  22.4 0.7 %copy.12 = f32[8,50,64]{2,0,1:T(8,128)} copy(f32[8,50,64]{2,0,1:T(8,128)S(1)} %bitcast.7) | data formatting | bytes 204800
  23.1 0.6 %copy.13 = f32[50,64]{1,0:T(8,128)} copy(f32[50,64]{1,0:T(8,128)S(1)} %get-tuple-element.9) | data formatting | bytes 25600
Async XLA Ops:
  0.6 1.5 %copy-start = (bf16[1,1000,4,128]{3,2,1,0:T(4,128)(2,1)S(1)}, bf16[1,1000,4,128]{3,2,1,0:T(4,128)(2,1)}, u32[]{:S(2)}) copy-start(bf16[1,1000,4,128]{3,2,1,0:T(4,128)(2,1)} %param.7) | copy-start | bytes 3072004
  0.6 1.5 %copy-start.1 = (f32[50,11,64]{2,0,1:T(8,128)S(1)}, f32[50,11,64]{2,0,1:T(8,128)}, u32[]{:S(2)}) copy-start(f32[50,11,64]{2,0,1:T(8,128)} %param.9) | copy-start | bytes 422404
  0.7 1.5 %copy-start.2 = (f32[10,528]{1,0:T(8,128)S(1)}, f32[10,528]{1,0:T(8,128)}, u32[]{:S(2)}) copy-start(f32[10,528]{1,0:T(8,128)} %basis_ref.1) | copy-start | bytes 63364
  0.7 1.5 %copy-start.3 = (s32[50]{0:T(128)S(1)}, s32[50]{0:T(128)}, u32[]{:S(2)}) copy-start(s32[50]{0:T(128)} %slot_s.1) | copy-start | bytes 604
  0.7 1.5 %copy-start.4 = (s32[50]{0:T(128)S(1)}, s32[50]{0:T(128)}, u32[]{:S(2)}) copy-start(s32[50]{0:T(128)} %shift_s.1) | copy-start | bytes 604
  0.7 1.5 %copy-start.5 = (s32[24]{0:T(128)S(1)}, s32[24]{0:T(128)}, u32[]{:S(2)}) copy-start(s32[24]{0:T(128)} %sky_s.1) | copy-start | bytes 292
